TPU v7x, 512 devices: a whole 4x4x16 slice. The times are simulated.
512 devices in a mesh: space: 64 (over x, z), tm: 8 (over y, core).
Axes of the slice: x: 4, y: 4, z: 16, core: 2. Of those that a mesh axis runs over, the one named last changes fastest.
Arguments:
- trajectory: float32 [64, 6, 65536], P('tm', None, 'space'), as said below
- counts: int32 [64, 64], P('space'), may hold values from 0 to 24, as said below
- particle_ids: int32 [65536], P('space'), may hold values from 0 to 196607, as said below
Outputs:
- coefficients: float32 [64, 6, 98304], P('tm', None, 'space')
- owned_ids: int32 [98304], P('space')
Inputs may be any that keep to these rules, and one draw needn't show every extreme that they name: `counts`: each row sums to 1024. Column pairs drawn from the seed split every region's rows: one owner of each pair gets 1024 // 64 plus some amount, the other that much less; one owner receives exactly 24 from every region. `particle_ids`: within a region's block the rows are grouped by owner in rising order; a row sent to owner o has an ID in [o * 3072, (o + 1) * 3072), and IDs rise within each region's block. `trajectory`: positions lie in [0, 4); velocity components within 0.3 of magnitude apart from small noise; the position change between snapshots stays far below half the box.
All inputs are finite; a program needn't handle non-finite values.
Results may differ from a plain program's by a relative error of at most 0.0003.
Values sent between devices are 32-bit elements; how exact they have to be, the bound alone decides.
A program may use at most 64 MiB of HBM per device.

v0:
```python
import jax
import jax.numpy as jnp
from jax import lax
from jax.sharding import PartitionSpec as P

LEVELS = 3


box_length = 4.0


def passed_along(block, axis, distance):
    devices = range(lax.axis_size(axis))
    route = [(i - distance, i) for i in devices if i - distance in devices]
    return lax.ppermute(block, axis, route)


def wrapped(delta):
    return delta - box_length * jnp.floor(delta / box_length + 0.5)


def hermite(start, finish, spacing):
    shift_pos = wrapped(finish[:, :3] - start[:, :3])
    guess_pos = start[:, :3] + 0.5 * shift_pos + 0.25 * spacing * (start[:, 3:] - finish[:, 3:])
    guess_vel = 0.75 * shift_pos / spacing - 0.25 * (start[:, 3:] + finish[:, 3:])
    return jnp.concatenate([guess_pos, guess_vel], axis=1)


def extrapolate(start, spacing):
    return jnp.concatenate([start[:, :3] + spacing * start[:, 3:], start[:, 3:]], axis=1)


def residue(odds, guess):
    return jnp.concatenate(
        [wrapped(odds[:, :3] - guess[:, :3]), odds[:, 3:] - guess[:, 3:]], axis=1
    )


def lift_block(block):
    first = lax.axis_index("tm") == 0
    final = lax.axis_index("tm") == lax.axis_size("tm") - 1
    for level in range(LEVELS):
        step = 2**level
        spacing = float(step)
        evens = block[0 :: 2 * step]
        odds = block[step :: 2 * step]
        after = passed_along(block[0:1], "tm", -1)
        rights = jnp.concatenate([evens[1:], after], axis=0)
        guess = hermite(evens, rights, spacing)
        tail = jnp.where(final, extrapolate(evens[-1:], spacing), guess[-1:])
        guess = jnp.concatenate([guess[:-1], tail], axis=0)
        detail = residue(odds, guess)
        before = passed_along(detail[-1:], "tm", 1)
        head = jnp.where(first, detail[:1], before)
        lefts = jnp.concatenate([head, detail[:-1]], axis=0)
        evens = evens + 0.25 * (lefts + detail)
        block = block.at[0 :: 2 * step].set(evens).at[step :: 2 * step].set(detail)
    return block


def regroup_rows(block, ids_local, counts_row):
    regions = counts_row.shape[1]
    rows = block.shape[2]
    width = 3 * rows // (2 * regions)
    amount = counts_row[0]
    offsets = jnp.cumsum(amount) - amount
    slot = jnp.arange(regions * width, dtype=jnp.int32)
    within = slot % width
    live = within < jnp.repeat(amount, width, total_repeat_length=regions * width)
    source = jnp.repeat(offsets, width, total_repeat_length=regions * width) + within
    source = jnp.where(live, source, 0)
    packed = jnp.where(live[None, None, :], jnp.take(block, source, axis=2), jnp.float32(0.0))
    tags = jnp.where(live, jnp.take(ids_local, source), -1)
    moved, owned = (
        lax.all_to_all(packed, "space", split_axis=2, concat_axis=2, tiled=True),
        lax.all_to_all(
            tags.reshape(1, 1, regions * width), "space", split_axis=2, concat_axis=2, tiled=True
        ),
    )
    return (moved, owned.reshape(regions * width))


def per_device(trajectory, counts, particle_ids):
    moved, owned_ids = regroup_rows(trajectory, particle_ids, counts)
    coefficients = lift_block(moved)
    return (coefficients, owned_ids)


def solution(mesh):
    in_specs = (P("tm", None, "space"), P("space", None), P("space"))
    out_specs = (P("tm", None, "space"), P("space"))
    return jax.shard_map(
        per_device, mesh=mesh, in_specs=in_specs, out_specs=out_specs, check_vma=False
    )
```

profile of v0, /device:TPU:14, one launch (start us, length us, event | category | flops | bytes accessed | tf_op | source)
XLA Modules:
  0.0 393.2 jit_solution(11214177452990771589)
XLA Ops:
  12.9 81.2 %compare_select_fusion = (s32[1536]{0:T(1024)S(1)}, pred[1536]{0:T(1024)(128)(4,1)S(1)}) fusion(pred[1536]{0:T(1024)(128)(4,1)} %constant.503, pred[1536]{0:T(1024)(128)(4,1)} %constant.504, pred[1536]{0:T(1024)(128)(4,1)} %constant.505, pred[1536]{0:T(1024)(128)(4,1)} %constant.506, pred[1536]{0:T(1024)(128)(4,1)} %constant.507, ...), kind=kLoop, calls=%fused_computation.78 | loop fusion | flops 211968 | bytes 104960 | tf_op jit(solution)/shard_map/jit(_take)/jit(_where)/select_n | solution.py:72
  94.2 3.7 copy.337
  97.9 5.8 %gather_fusion.1 = s32[1536]{0:T(1024)S(1)} fusion(s32[1024]{0:T(1024)S(1)} %copy-done, s32[2048]{0:T(1024)S(1)} %pad_clamp_fusion), kind=kCustom, calls=%fused_computation.1 | custom fusion | bytes 18432 | tf_op jit(solution)/shard_map/jit(_take)/gather | solution.py:73
  103.7 6.7 %gather_fusion = f32[1536,8,6]{2,1,0:T(8,128)} fusion(f32[8,6,1024]{1,0,2:T(8,128)} %copy.337, s32[2048]{0:T(1024)S(1)} %pad_clamp_fusion), kind=kCustom, calls=%fused_computation | custom fusion | bytes 595968 | tf_op jit(solution)/shard_map/jit(_take)/gather | solution.py:72
  110.4 9.7 %select_bitcast_fusion = f32[8,6,1536]{1,0,2:T(8,128)} fusion(f32[1536,8,6]{2,1,0:T(8,128)} %gather_fusion, pred[1536]{0:T(1024)(128)(4,1)S(1)} %get-tuple-element.68, pred[1536]{0:T(1024)(128)(4,1)S(1)} %get-tuple-element.60), kind=kLoop, calls=%fused_computation.6 | loop fusion | flops 147456 | bytes 592896 | tf_op jit(solution)/shard_map/jit(_where)/select_n | solution.py:72
  120.1 12.0 %copy.338 = f32[8,6,1536]{0,1,2:T(8,128)} copy(f32[8,6,1536]{1,0,2:T(8,128)} %select_bitcast_fusion) | data formatting | bytes 589824 | tf_op jit(solution)/shard_map/jit(_where)/select_n | solution.py:72
  132.1 5.4 %reshape.550 = f32[64,1,1152]{2,1,0:T(1,128)} reshape(f32[1536,6,8]{2,1,0:T(8,128)} %bitcast.152) | data formatting | bytes 589824
  137.4 18.8 %all-to-all-start = ((f32[64,1,1152]{2,1,0:T(1,128)}), f32[64,1,1152]{2,1,0:T(1,128)S(1)}, u32[]{:S(2)}, u32[]{:S(2)}) async-start(f32[64,1,1152]{2,1,0:T(1,128)} %reshape.550), calls=%async_computation | async-start | bytes 589824 | tf_op jit(solution)/shard_map/all_to_all | solution.py:75
  157.4 21.1 %all-to-all-done = f32[64,1,1152]{2,1,0:T(1,128)S(1)} async-done(((f32[64,1,1152]{2,1,0:T(1,128)}), f32[64,1,1152]{2,1,0:T(1,128)S(1)}, u32[]{:S(2)}, u32[]{:S(2)}) %all-to-all-start) | async-done | bytes 294944 | tf_op jit(solution)/shard_map/all_to_all | solution.py:75
  180.3 4.4 %reshape.551 = f32[1536,6,8]{2,1,0:T(8,128)} reshape(f32[64,1152]{1,0:T(8,128)S(1)} %reduce.9) | data formatting | bytes 589824
  184.7 32.0 %slice.230 = f32[4,6,1536]{0,1,2:T(8,128)} slice(f32[8,6,1536]{0,1,2:T(8,128)} %bitcast.148), slice={[0:8:2], [0:6:1], [0:1536:1]} | slice | bytes 294912 | tf_op jit(solution)/shard_map/slice | solution.py:45
  216.7 32.5 %slice.231 = f32[4,6,1536]{0,1,2:T(8,128)} slice(f32[8,6,1536]{0,1,2:T(8,128)} %bitcast.149), slice={[1:8:2], [0:6:1], [0:1536:1]} | slice | bytes 294912 | tf_op jit(solution)/shard_map/slice | solution.py:46
  249.2 4.8 %copy.341 = f32[1,6,1536]{2,0,1:T(1,128)} copy(f32[1,6,1536]{0,1,2:T(8,128)} %bitcast.150) | data formatting | bytes 73728 | tf_op jit(solution)/shard_map/slice | solution.py:47
  256.1 4.2 %copy.359 = f32[4,6,1536]{2,0,1:T(4,128)S(1)} copy(f32[4,6,1536]{0,1,2:T(8,128)} %slice.230) | data formatting | bytes 294912
  260.3 7.1 %fusion.30 = (f32[4,3,1536]{0,1,2:T(4,128)}, f32[4,3,1536]{0,1,2:T(4,128)S(1)}) fusion(f32[4,6,1536]{0,1,2:T(8,128)} %slice.231), kind=kLoop, calls=%fused_computation.107 | loop fusion | bytes 294912 | tf_op jit(solution)/shard_map/slice | solution.py:35
  268.0 4.4 %copy.342 = f32[8,6,1536]{2,1,0:T(8,128)S(1)} copy(f32[8,6,1536]{0,1,2:T(8,128)} %bitcast.151) | data formatting | bytes 589824 | tf_op jit(solution)/shard_map/all_to_all | solution.py:75
  274.1 3.6 copy.362
  282.8 2.4 collective-permute-start.1
  285.2 2.8 collective-permute-done.1
  294.9 3.6 collective-permute-start.3
  305.6 3.6 collective-permute-start.5
  309.3 4.6 %reshape.547 = s32[1,1,1536]{1,0,2:T(1,128)S(1)} reshape(s32[1536]{0:T(1024)S(1)} %get-tuple-element.59) | data formatting | bytes 12288 | tf_op jit(solution)/shard_map/reshape | solution.py:77
  313.8 49.3 %all_to_all.10 = s32[1,1,1536]{1,0,2:T(1,128)S(1)} all-to-all(s32[1,1,1536]{1,0,2:T(1,128)S(1)} %reshape.547), channel_id=1, replica_groups=mesh['space'=64,'tm'=8] {'space'}, dimensions={2} | all-to-all | bytes 12288 | tf_op jit(solution)/shard_map/all_to_all | solution.py:76
  363.2 29.1 %reduce.8 = s32[1536]{0:T(1024)} reduce(s32[1,1,1536]{1,0,2:T(1,128)S(1)} %all_to_all.10, s32[]{:T(128)} %constant.222.clone.1), dimensions={0,1}, to_apply=%all_to_all.7.reduce_sub_computation | reduce | bytes 12292 | tf_op jit(solution)/shard_map/all_to_all | solution.py:76
  (77 shorter events, 39.5 us)
Async XLA Ops:
  0.6 97.2 %copy-start = (s32[1024]{0:T(1024)S(1)}, s32[1024]{0:T(1024)}, u32[]{:S(2)}) copy-start(s32[1024]{0:T(1024)} %param.15) | copy-start | bytes 12292
  137.4 41.0 %all-to-all-start = ((f32[64,1,1152]{2,1,0:T(1,128)}), f32[64,1,1152]{2,1,0:T(1,128)S(1)}, u32[]{:S(2)}, u32[]{:S(2)}) async-start(f32[64,1,1152]{2,1,0:T(1,128)} %reshape.550), calls=%async_computation | async-start | bytes 589824 | tf_op jit(solution)/shard_map/all_to_all | solution.py:75
  254.0 25.6 %collective-permute-start = (f32[1,6,1536]{2,0,1:T(1,128)}, f32[1,6,1536]{2,0,1:T(1,128)}, u32[]{:S(2)}, u32[]{:S(2)}) collective-permute-start(f32[1,6,1536]{2,0,1:T(1,128)} %copy.341), channel_id=1, source_target_pairs={{1,0},{2,1},{3,2},{4,3},{5,4},{6,5},{7,6},{9,8},{10,9},{11,10},{12... | collective-permute-start | bytes 110600 | tf_op jit(solution)/shard_map/ppermute | solution.py:15
  260.3 7.1 %copy-start.1 = (f32[4,6,1536]{2,0,1:T(4,128)}, f32[4,6,1536]{2,0,1:T(4,128)S(1)}, u32[]{:S(2)}) copy-start(f32[4,6,1536]{2,0,1:T(4,128)S(1)} %copy.359) | copy-start | bytes 442372
  282.8 5.3 %collective-permute-start.1 = (f32[1,6,1536]{2,0,1:T(1,128)S(1)}, f32[1,6,1536]{2,0,1:T(1,128)S(1)}, u32[]{:S(2)}, u32[]{:S(2)}) collective-permute-start(f32[1,6,1536]{2,0,1:T(1,128)S(1)} %fusion.21), channel_id=1, source_target_pairs={{0,1},{1,2},{2,3},{3,4},{4,5},{5,6},{6,7},{8,9},{9,10},{10,11},{11... | collective-permute-start | bytes 110600 | tf_op jit(solution)/shard_map/ppermute | solution.py:15
  290.9 3.5 collective-permute-start.2
  294.9 5.3 %collective-permute-start.3 = (f32[1,6,1536]{2,0,1:T(1,128)S(1)}, f32[1,6,1536]{2,0,1:T(1,128)S(1)}, u32[]{:S(2)}, u32[]{:S(2)}) collective-permute-start(f32[1,6,1536]{2,0,1:T(1,128)S(1)} %fusion.19), channel_id=1, source_target_pairs={{0,1},{1,2},{2,3},{3,4},{4,5},{5,6},{6,7},{8,9},{9,10},{10,11},{11... | collective-permute-start | bytes 110600 | tf_op jit(solution)/shard_map/ppermute | solution.py:15
  301.8 3.5 collective-permute-start.4
  305.6 86.6 %collective-permute-start.5 = (f32[1,6,1536]{2,0,1:T(1,128)S(1)}, f32[1,6,1536]{2,0,1:T(1,128)S(1)}, u32[]{:S(2)}, u32[]{:S(2)}) collective-permute-start(f32[1,6,1536]{2,0,1:T(1,128)S(1)} %pad_maximum_fusion.8), channel_id=1, source_target_pairs={{0,1},{1,2},{2,3},{3,4},{4,5},{5,6},{6,7},{8,9},{9,10},{10,11},{11... | collective-permute-start | bytes 110600 | tf_op jit(solution)/shard_map/ppermute | solution.py:15
where the time goes:
time: 398 us; the launch traced here: 393 us
  local copies, waits for them, and re-layouts  151 us (38%)
  other arithmetic  129 us (32%)
  blocking collectives  49.3 us (12%)
  starting transfers between devices  34.3 us (9%)
  waiting for transfers between devices  28.6 us (7%)
    select_n x1, other arithmetic, regroup_rows(): jnp.take(block, source, axis=2)  81.2 us
    all_to_all x1, blocking collectives, regroup_rows(): lax.all_to_all(tags.reshape(1, 1, regions * width), 'space', split_axis=2...  49.3 us
    slice x2, local copies, waits for them, and re-layouts, lift_block(): odds = block[step::2 * step]  32.5 us
    slice x2, local copies, waits for them, and re-layouts, lift_block(): evens = block[0::2 * step]  32 us
    all_to_all x1, other arithmetic, regroup_rows(): lax.all_to_all(tags.reshape(1, 1, regions * width), 'space', split_axis=2...  29.1 us
    unnamed x13, local copies, waits for them, and re-layouts  24.1 us
    all_to_all x1, waiting for transfers between devices, regroup_rows(): lax.all_to_all(packed, 'space', split_axis=2, concat_axis=2, tiled=True)  21.1 us
    all_to_all x1, starting transfers between devices, regroup_rows(): lax.all_to_all(packed, 'space', split_axis=2, concat_axis=2, tiled=True)  18.8 us
  transfers between devices with their start and end apart: 7, of which 5 were waited for; matrix products, arithmetic and copies ran while one was open for 15% of the time, Pallas kernels for 0%

commit v1 on v0

v1 whole, which is shorter than its diff:
```python
import functools

import jax
import jax.numpy as jnp
from jax import lax
from jax.experimental import pallas as pl
from jax.experimental.pallas import tpu as pltpu
from jax.sharding import PartitionSpec as P

MESH = pl.DeviceIdType.MESH
NX = 4
NZ = 16
NT = 8
CAP = 24
ROWS = 1024
LANES = 128
WIDE = NZ * CAP
CHUNK = 256
REACH = 4
NEAR = (4, 12, 3, 13, 2, 14, 1, 15)
FAR = (8, 7, 9, 6, 10, 5, 11)
FAR_FIRST = FAR + NEAR
TILES1 = 2
TILES2 = 3


def wrapped(delta):
    return delta - 4.0 * jnp.floor(delta * 0.25 + 0.5)


def detail_of(start, odd, finish, h, final=None):
    (xa, va), (xo, vo), (xb, vb) = start, odd, finish
    shift = wrapped(xb - xa)
    guess_x = xa + 0.5 * shift + (0.25 * h) * (va - vb)
    guess_v = (0.75 / h) * shift - 0.25 * (va + vb)
    if final is not None:
        guess_x = jnp.where(final, xa + h * va, guess_x)
        guess_v = jnp.where(final, va, guess_v)
    return wrapped(xo - guess_x), vo - guess_v


def updated(even, left, right):
    return tuple(e + 0.25 * (a + b) for e, a, b in zip(even, left, right))


def chosen(flag, a, b):
    return tuple(jnp.where(flag, p, q) for p, q in zip(a, b))


def kernel(
    counts_hbm, ids_hbm, traj, coef, oid,
    counts, ids, x, s1, s2, to_left, to_right, from_right, from_left, edge, edge_in,
    zs1, zs2, zr1, zr2, tail, u1, u2, a1, a2, aid, offs,
    load_sem, far_sem, halo_s, halo_r, z_s1, z_r1, z_s2, z_r2, x_s, x_r,
):
    me = lax.axis_index("space")
    mx, mz = me // NZ, me % NZ
    mt = lax.axis_index("tm")
    first, final = mt == 0, mt == NT - 1
    left, right = (mt + NT - 1) % NT, (mt + 1) % NT

    def z_peer(k):
        z = (mz + k) % NZ
        return z, {"space": mx * NZ + z}

    def x_peer(k):
        xp = (mx + k) % NX
        return xp, {"space": xp * NZ + mz}

    barrier = pltpu.get_barrier_semaphore()
    peers = [z_peer(k)[1] for k in NEAR] + [x_peer(k)[1] for k in range(1, NX)]
    peers += [{"tm": left}, {"tm": right}]
    for peer in peers:
        pl.semaphore_signal(barrier, inc=1, device_id=peer, device_id_type=MESH)

    loads = [
        pltpu.make_async_copy(counts_hbm, counts, load_sem.at[0]),
        pltpu.make_async_copy(traj, x, load_sem.at[1]),
        pltpu.make_async_copy(ids_hbm, ids, load_sem.at[2]),
    ]
    for load in loads:
        load.start()
    loads[0].wait()
    total = jnp.int32(0)
    for o in range(NX * NZ):
        offs[o] = total
        total = total + counts[0, o]
    loads[1].wait()
    loads[2].wait()

    def snap(i, lanes):
        return x[0:3, i, lanes], x[3:6, i, lanes]

    def pair(ref, i, lanes):
        return ref[6 * i : 6 * i + 3, lanes], ref[6 * i + 3 : 6 * i + 6, lanes]

    def put(ref, i, lanes, value):
        ref[6 * i : 6 * i + 3, lanes], ref[6 * i + 3 : 6 * i + 6, lanes] = value

    for c in range(ROWS // CHUNK):
        lanes = slice(c * CHUNK, (c + 1) * CHUNK)
        p = [snap(i, lanes) for i in range(8)]
        d1 = detail_of(p[0], p[1], p[2], 1.0)
        d3 = detail_of(p[2], p[3], p[4], 1.0)
        d5 = detail_of(p[4], p[5], p[6], 1.0)
        e2 = updated(p[2], d1, d3)
        e4 = updated(p[4], d3, d5)
        for i, v in enumerate((d1, d3, d5)):
            put(s1, i, lanes, v)
        s1[18:20, lanes] = d5[1][1:3]
        s1[20:24, lanes] = jnp.zeros((4, CHUNK), jnp.float32)
        for i, v in enumerate((p[0], d1, e2, e4)):
            put(to_left, i, lanes, v)
        for i, v in enumerate((e4, d5, p[6], p[7])):
            put(to_right, i, lanes, v)
        s2[30:31, lanes] = (ids[0:1, lanes] + 1).astype(jnp.float32)
        s2[31:32, lanes] = jnp.zeros((1, CHUNK), jnp.float32)

    lane = lax.broadcasted_iota(jnp.int32, (8, LANES), 1)
    row = lax.broadcasted_iota(jnp.int32, (8, LANES), 0)

    def window(o):
        owners = NX * NZ
        low = max(0, ROWS - CAP * (owners - o))
        high = min(CAP * o, ROWS - 1)
        tiles = range(low // LANES, min(high + CAP - 1, ROWS - 1) // LANES + 1)
        off = offs[o]
        tile = (off >> 7) + (lane < (off & (LANES - 1))).astype(jnp.int32)
        return tiles, tile, off, counts[0, o]

    def taken(src, strip, tiles, tile, index):
        rows = slice(8 * strip, 8 * strip + 8)
        block = src[rows, tiles[0] * LANES : (tiles[0] + 1) * LANES]
        for t in tiles[1:]:
            block = jnp.where(tile == t, src[rows, t * LANES : (t + 1) * LANES], block)
        return jnp.take_along_axis(block, index, axis=1, mode="promise_in_bounds")

    def pack(src, full, z, last_apart):
        out = [jnp.zeros((8, LANES), jnp.float32) for _ in range(full)]
        apart = []
        for xp in range(NX):
            tiles, tile, off, count = window(xp * NZ + z)
            begin = xp * CAP
            index = (lane + (off - begin)) & (LANES - 1)
            live = (lane >= begin) & (lane < begin + count)
            for strip in range(full):
                out[strip] = jnp.where(live, taken(src, strip, tiles, tile, index), out[strip])
            if last_apart:
                begin = NX * CAP
                index = (lane + (off - begin)) & (LANES - 1)
                live = (lane >= begin) & (lane < begin + count)
                apart.append(jnp.where(live, taken(src, full, tiles, tile, index), 0.0))
        return out, apart

    spare = lane >= NX * CAP
    for z in range(NZ):
        out, apart = pack(s1, TILES1, z, True)
        for i in range(TILES1):
            zs1[z, 8 * i : 8 * i + 8, :] = jnp.where(
                spare, jnp.where(row < 2, apart[i], apart[i + 2]), out[i]
            )

    def remote(src, dst, send, recv, peer):
        return pltpu.make_async_remote_copy(
            src_ref=src, dst_ref=dst, send_sem=send, recv_sem=recv, device_id=peer, device_id_type=MESH
        )

    halos = [
        remote(to_left, from_right, halo_s.at[0], halo_r.at[0], {"tm": left}),
        remote(to_right, from_left, halo_s.at[1], halo_r.at[1], {"tm": right}),
        remote(edge, edge_in, halo_s.at[2], halo_r.at[2], {"tm": right}),
    ]

    def z_send(k, zs, zr, send, recv):
        z, peer = z_peer(k)
        return remote(zs.at[z], zr.at[mz], send.at[z], recv.at[mz], peer)

    def z_arrival(k, zs, zr, send, recv):
        z, peer = z_peer(k)
        return remote(zs.at[z], zr.at[z], send.at[z], recv.at[z], peer)

    pl.semaphore_wait(barrier, len(peers))
    for k in (REACH, NZ - REACH):
        pl.semaphore_signal(far_sem, inc=1, device_id=z_peer(k)[1], device_id_type=MESH)
    halos[0].start()
    halos[1].start()
    for k in NEAR:
        z_send(k, zs1, zr1, z_s1, z_r1).start()
    pl.semaphore_wait(far_sem, 2)
    for k in FAR:
        z_send(k, zs1, zr1, z_s1, z_r1).start()
    zr1[mz] = zs1[mz]

    halos[0].wait_recv()
    halos[1].wait_recv()

    for c in range(ROWS // CHUNK):
        lanes = slice(c * CHUNK, (c + 1) * CHUNK)
        x0, d1, e2, e4 = (pair(to_left, i, lanes) for i in range(4))
        d5, x6, x7 = (pair(to_right, i, lanes) for i in range(1, 4))
        x8, d9, e10, e12 = (pair(from_right, i, lanes) for i in range(4))
        em4, dm3, xm2, xm1 = (pair(from_left, i, lanes) for i in range(4))
        dm1 = detail_of(xm2, xm1, x0, 1.0)
        e0 = updated(x0, chosen(first, d1, dm1), d1)
        d7 = detail_of(x6, x7, x8, 1.0, final)
        e6 = updated(x6, d5, d7)
        e8 = updated(x8, d7, d9)
        em2 = updated(xm2, dm3, dm1)
        dm2 = detail_of(em4, em2, e0, 2.0)
        d2 = detail_of(e0, e2, e4, 2.0)
        d6 = detail_of(e4, e6, e8, 2.0, final)
        d10 = detail_of(e8, e10, e12, 2.0)
        f0 = updated(e0, chosen(first, d2, dm2), d2)
        f4 = updated(e4, d2, d6)
        f8 = updated(e8, d6, d10)
        d4 = detail_of(f0, f4, f8, 4.0, final)
        for i, v in enumerate((f0, d2, d4, d6, d7)):
            put(s2, i, lanes, v)
        put(edge, 0, lanes, d4)

    halos[2].start()
    halos[2].wait_recv()

    d4 = edge[...]
    before = jnp.where(first, d4, edge_in[...])
    s2[0:6, :] = s2[0:6, :] + 0.25 * (before + d4)

    for z in range(NZ):
        out, _ = pack(s2, TILES2 + 1, z, False)
        for i in range(TILES2):
            moved = pltpu.roll(out[TILES2], NX * CAP - 32 * i, 1)
            zs2[z, 8 * i : 8 * i + 8, :] = jnp.where(spare, moved, out[i])
    for k in FAR_FIRST:
        z_send(k, zs2, zr2, z_s2, z_r2).start()
    zr2[mz] = zs2[mz]

    def placed(u, strip, part):
        rows = slice(8 * strip, 8 * strip + 8)
        for xp in range(NX):
            tiles = [None] * (WIDE // LANES)
            for z in range(NZ):
                block, begin = part(z, xp)
                turn = (z * CAP - begin) % LANES
                turned = pltpu.roll(block, turn, 1) if turn else block
                for t in range(WIDE // LANES):
                    low, high = z * CAP - t * LANES, (z + 1) * CAP - t * LANES
                    if high > 0 and low < LANES:
                        old = tiles[t]
                        tiles[t] = turned if old is None else jnp.where(lane >= low, turned, old)
            for t in range(WIDE // LANES):
                u[xp, rows, t * LANES : (t + 1) * LANES] = tiles[t]

    own = pl.ds(pl.multiple_of(mx * WIDE, LANES), WIDE)

    def lanes_from(xp):
        return pl.ds(pl.multiple_of(xp * WIDE, LANES), WIDE)

    def parts(xp, here):
        return (
            (a1.at[xp], coef.at[0:3, 1, :, here]),
            (a2.at[xp, 0:4], coef.at[0:4, 0, :, here]),
            (a2.at[xp, 4], coef.at[3, 1, :, here]),
            (aid.at[xp], oid.at[:, here]),
        )

    def to_owner(k, i):
        xp, peer = x_peer(k)
        src, dst = parts(xp, own)[i]
        return remote(src, dst, x_s.at[k, i], x_r.at[k, i], peer)

    def from_region(k, i):
        xp, peer = x_peer(NX - k)
        src, dst = parts(xp, lanes_from(xp))[i]
        return remote(src, dst, x_s.at[k, i], x_r.at[k, i], peer)

    for k in FAR_FIRST:
        z_arrival(k, zs1, zr1, z_s1, z_r1).wait_recv()
    for strip in range(TILES1):
        placed(u1, strip, lambda z, xp: (zr1[z, 8 * strip : 8 * strip + 8, :], xp * CAP))
    placed(u1, TILES1, lambda z, xp: (zr1[z, 8 * (xp % 2) : 8 * (xp % 2) + 8, :], NX * CAP))
    for xp in range(NX):
        a1[xp, 0] = u1[xp, 0:6, :]
        a1[xp, 1] = u1[xp, 6:12, :]
        a1[xp, 2, 0:4] = u1[xp, 12:16, :]
        last = 16 + 2 * (xp // 2)
        a1[xp, 2, 4:6] = u1[xp, last : last + 2, :]
    for k in (2, 1, 3):
        to_owner(k, 0).start()
    coef[0:3, 1, :, own] = a1[mx]

    for k in FAR_FIRST:
        z_arrival(k, zs2, zr2, z_s2, z_r2).wait_recv()
    for strip in range(TILES2):
        placed(u2, strip, lambda z, xp: (zr2[z, 8 * strip : 8 * strip + 8, :], xp * CAP))
    for z in range(NZ):
        whole = pltpu.roll(zr2[z, 0:8, :], 32, 1)
        whole = jnp.where(lane < 32, whole, pltpu.roll(zr2[z, 8:16, :], 64, 1))
        last = jnp.where(lane < 64, whole, pltpu.roll(zr2[z, 16:24, :], 96, 1))
        tail[z] = last
    placed(u2, TILES2, lambda z, xp: (tail[z], xp * CAP))
    for xp in range(NX):
        for i in range(5):
            a2[xp, i] = u2[xp, 6 * i : 6 * i + 6, :]
        aid[xp] = u2[xp, 30:31, :].astype(jnp.int32) - 1
    for i in (1, 2, 3):
        for k in (2, 1, 3):
            to_owner(k, i).start()
    coef[0:4, 0, :, own] = a2[mx, 0:4]
    coef[3, 1, :, own] = a2[mx, 4]
    oid[:, own] = aid[mx]

    for k in (2, 1, 3):
        for i in range(4):
            from_region(k, i).wait_recv()
    for halo in halos:
        halo.wait_send()
    for k in FAR_FIRST:
        z_send(k, zs1, zr1, z_s1, z_r1).wait_send()
        z_send(k, zs2, zr2, z_s2, z_r2).wait_send()
    for k in (2, 1, 3):
        for i in range(4):
            to_owner(k, i).wait_send()


def per_device(trajectory, counts, particle_ids):
    f32, i32 = jnp.float32, jnp.int32
    vmem = lambda *shape: pltpu.VMEM(shape, f32)
    dma = pltpu.SemaphoreType.DMA
    slots = NX * WIDE
    coefficients, owned = pl.pallas_call(
        kernel,
        out_shape=(
            jax.ShapeDtypeStruct((4, 2, 6, slots), f32),
            jax.ShapeDtypeStruct((1, slots), i32),
        ),
        in_specs=[pl.BlockSpec(memory_space=pltpu.HBM)] * 3,
        out_specs=(pl.BlockSpec(memory_space=pltpu.VMEM), pl.BlockSpec(memory_space=pltpu.VMEM)),
        scratch_shapes=[
            pltpu.SMEM((1, NX * NZ), i32), pltpu.VMEM((1, ROWS), i32), vmem(6, 8, ROWS),
            vmem(24, ROWS), vmem(32, ROWS),
            vmem(24, ROWS), vmem(24, ROWS), vmem(24, ROWS), vmem(24, ROWS),
            vmem(6, ROWS), vmem(6, ROWS),
            vmem(NZ, 8 * TILES1, LANES), vmem(NZ, 8 * TILES2, LANES),
            vmem(NZ, 8 * TILES1, LANES), vmem(NZ, 8 * TILES2, LANES), vmem(NZ, 8, LANES),
            vmem(NX, 24, WIDE), vmem(NX, 32, WIDE),
            vmem(NX, 3, 6, WIDE), vmem(NX, 5, 6, WIDE),
            pltpu.VMEM((NX, 1, WIDE), i32), pltpu.SMEM((NX * NZ,), i32),
            dma((3,)), pltpu.SemaphoreType.REGULAR, dma((3,)), dma((3,)),
            dma((NZ,)), dma((NZ,)), dma((NZ,)), dma((NZ,)), dma((NX, 4)), dma((NX, 4)),
        ],
        compiler_params=pltpu.CompilerParams(
            collective_id=0, has_side_effects=True, vmem_limit_bytes=60 * 2**20
        ),
        name="regroup_and_lift",
    )(counts, particle_ids.reshape(1, ROWS), trajectory.transpose(1, 0, 2))
    return coefficients.reshape(8, 6, slots), owned.reshape(slots)


def solution(mesh):
    return jax.shard_map(
        per_device,
        mesh=mesh,
        in_specs=(P("tm", None, "space"), P("space", None), P("space")),
        out_specs=(P("tm", None, "space"), P("space")),
        check_vma=False,
    )
```

time: 398 us -> 42 us (0.11)
  the two profiles are of different devices: /device:TPU:14 before, /device:TPU:16 now
where the time goes in v1:
time: 42 us; the launch traced here: 41.9 us
  Pallas kernels  38.7 us (92%)
  local copies, waits for them, and re-layouts  1.89 us (4%)
  between operations  0.65 us (2%)
  other arithmetic  0.62 us (1%)
    pallas_call x1, Pallas kernels, per_device(): pl.pallas_call(kernel, out_shape=(jax.ShapeDtypeStruct((4, 2, 6, slots),...  38.7 us
    unnamed x3, local copies, waits for them, and re-layouts  1.89 us

profile of v1, /device:TPU:16, one launch (start us, length us, event | category | flops | bytes accessed | tf_op | source)
XLA Modules:
  0.0 41.9 jit_solution(12989453023140428079)
XLA Ops:
  0.6 38.7 %regroup_and_lift.1 = (f32[4,2,6,1536]{3,2,1,0:T(8,128)}, s32[1,1536]{1,0:T(1,128)}) custom-call(s32[1,64]{1,0:T(1,128)} %counts_hbm.1, s32[1,1024]{1,0:T(1,128)} %bitcast.5, f32[6,8,1024]{2,1,0:T(8,128)} %bitcast.4), custom_call_target="tpu_custom_call" | custom-call | tf_op jit(solution)/shard_map/regroup_and_lift/pallas_call | solution.py:330
  39.3 0.0 copy-start
  39.4 1.9 %copy.5 = f32[8,6,1536]{2,0,1:T(8,128)} copy(f32[8,6,1536]{2,1,0:T(8,128)} %bitcast.3) | data formatting | bytes 589824
  41.2 0.0 copy-done
  41.2 0.6 %reduce = s32[1536]{0:T(1024)} reduce(s32[1,1536]{1,0:T(1,128)S(1)} %copy-done, s32[]{:T(128)} %constant.1), dimensions={0}, to_apply=%get-tuple-element.5.reduce_sub_computation | reduce | bytes 12292 | tf_op jit(solution)/shard_map/regroup_and_lift/pallas_call | solution.py:330
Async XLA Ops:
  39.3 1.9 %copy-start = (s32[1,1536]{1,0:T(1,128)S(1)}, s32[1,1536]{1,0:T(1,128)}, u32[]{:S(2)}) copy-start(s32[1,1536]{1,0:T(1,128)} %get-tuple-element.5) | copy-start | bytes 18436

commit v2 on v1

v2 whole, which is shorter than its diff:
```python
import functools

import jax
import jax.numpy as jnp
from jax import lax
from jax.experimental import pallas as pl
from jax.experimental.pallas import tpu as pltpu
from jax.sharding import PartitionSpec as P

MESH = pl.DeviceIdType.MESH
NX = 4
NZ = 16
NT = 8
CAP = 24
ROWS = 1024
LANES = 128
SLOT_TILES = NX * NZ * CAP // LANES
WIDE = NZ * CAP
X_TILES = WIDE // LANES
CHUNK = 256
X_ORDER = (2, 1, 3)
REACH = 4
NEAR = (4, 12, 3, 13, 2, 14, 1, 15)
FAR = (5, 11, 6, 10, 7, 9, 8)
FAR_FIRST = (8, 7, 9, 6, 10, 5, 11) + NEAR
SPAN = NX * CAP
PHASES = ((24, 2), (24, 2), (8, 1))


def wrapped(delta):
    return delta - 4.0 * jnp.floor(delta * 0.25 + 0.5)


def detail_of(start, odd, finish, h, final=None):
    (xa, va), (xo, vo), (xb, vb) = start, odd, finish
    shift = wrapped(xb - xa)
    guess_x = xa + 0.5 * shift + (0.25 * h) * (va - vb)
    guess_v = (0.75 / h) * shift - 0.25 * (va + vb)
    if final is not None:
        guess_x = jnp.where(final, xa + h * va, guess_x)
        guess_v = jnp.where(final, va, guess_v)
    return wrapped(xo - guess_x), vo - guess_v


def updated(even, left, right):
    return tuple(e + 0.25 * (a + b) for e, a, b in zip(even, left, right))


def chosen(flag, a, b):
    return tuple(jnp.where(flag, p, q) for p, q in zip(a, b))


def kernel(
    counts_hbm, ids_hbm, traj, coef, oid,
    counts, ids, x, s0, s1, s2, to_left, to_right, from_right, from_left, edge, edge_in,
    index, place, offs, xs0, xs1, xs2, xr0, xr1, xr2, zs0, zs1, zs2, zr0, zr1, zr2, tail, u0, u1, w0,
    load_sem, far_sem, halo_s, halo_r, z_s, z_r, x_s, x_r,
):
    me = lax.axis_index("space")
    mx, mz = me // NZ, me % NZ
    mt = lax.axis_index("tm")
    first, final = mt == 0, mt == NT - 1
    left, right = (mt + NT - 1) % NT, (mt + 1) % NT
    rows_of, xs, xr = (s0, s1, s2), (xs0, xs1, xs2), (xr0, xr1, xr2)
    zs, zr = (zs0, zs1, zs2), (zr0, zr1, zr2)

    def z_peer(k):
        z = (mz + k) % NZ
        return z, {"space": mx * NZ + z}

    def x_peer(k):
        xp = (mx + k) % NX
        return xp, {"space": xp * NZ + mz}

    barrier = pltpu.get_barrier_semaphore()
    peers = [z_peer(k)[1] for k in NEAR] + [x_peer(k)[1] for k in X_ORDER]
    peers += [{"tm": left}, {"tm": right}]
    for peer in peers:
        pl.semaphore_signal(barrier, inc=1, device_id=peer, device_id_type=MESH)

    loads = [
        pltpu.make_async_copy(counts_hbm, counts, load_sem.at[0]),
        pltpu.make_async_copy(traj, x, load_sem.at[1]),
        pltpu.make_async_copy(ids_hbm, ids, load_sem.at[2]),
    ]
    for load in loads:
        load.start()
    loads[0].wait()
    total = jnp.int32(0)
    for o in range(NX * NZ):
        offs[o] = total
        total = total + counts[0, o]

    lane = lax.broadcasted_iota(jnp.int32, (8, LANES), 1)
    row = lax.broadcasted_iota(jnp.int32, (8, LANES), 0)
    spare = lane >= SPAN

    for t in range(SLOT_TILES):
        base = t * LANES
        o0 = base // CAP
        shift, end = None, None
        for o in range(o0, (base + LANES - 1) // CAP + 1):
            begin = o * CAP - base
            shift_o, end_o = offs[o] - begin, begin + counts[0, o]
            if shift is None:
                shift, end = jnp.full((8, LANES), shift_o), jnp.full((8, LANES), end_o)
            else:
                shift, end = jnp.where(lane >= begin, shift_o, shift), jnp.where(lane >= begin, end_o, end)
        index[t] = jnp.where(lane < end, (lane + shift) & (LANES - 1), -1)
        start = offs[o0] + jnp.minimum(base - o0 * CAP, counts[0, o0])
        place[t] = (start >> 7) + (lane < (start & (LANES - 1))).astype(jnp.int32)

    loads[1].wait()
    loads[2].wait()

    def snap(i, lanes):
        return x[0:3, i, lanes], x[3:6, i, lanes]

    def pair(ref, i, lanes):
        return ref[6 * i : 6 * i + 3, lanes], ref[6 * i + 3 : 6 * i + 6, lanes]

    def put(ref, i, lanes, value):
        ref[6 * i : 6 * i + 3, lanes], ref[6 * i + 3 : 6 * i + 6, lanes] = value

    for c in range(ROWS // CHUNK):
        lanes = slice(c * CHUNK, (c + 1) * CHUNK)
        p = [snap(i, lanes) for i in range(8)]
        d1 = detail_of(p[0], p[1], p[2], 1.0)
        d3 = detail_of(p[2], p[3], p[4], 1.0)
        d5 = detail_of(p[4], p[5], p[6], 1.0)
        e2 = updated(p[2], d1, d3)
        e4 = updated(p[4], d3, d5)
        for i, v in enumerate((p[0], d1, e2, e4)):
            put(to_left, i, lanes, v)
        for i, v in enumerate((e4, d5, p[6], p[7])):
            put(to_right, i, lanes, v)
        for i, v in enumerate((d1, d3, d5)):
            put(s0, i, lanes, v)
        s0[18:20, lanes] = d5[1][1:3]
        s0[20:24, lanes] = jnp.zeros((4, CHUNK), jnp.float32)
        s2[6:7, lanes] = (ids[0:1, lanes] + 1).astype(jnp.float32)
        s2[7:8, lanes] = jnp.zeros((1, CHUNK), jnp.float32)

    def pack(phase):
        src, dst = rows_of[phase], xs[phase]
        strips = PHASES[phase][0] // 8
        for t in range(SLOT_TILES):
            slots = index[t]
            live = slots >= 0
            slots = slots & (LANES - 1)
            where = place[t]
            low = max(0, (ROWS - (SLOT_TILES - t) * LANES) // LANES)
            high = min(t, ROWS // LANES - 1)
            lanes = slice((t % X_TILES) * LANES, (t % X_TILES + 1) * LANES)
            for strip in range(strips):
                rows = slice(8 * strip, 8 * strip + 8)
                block = src[rows, low * LANES : (low + 1) * LANES]
                for i in range(low + 1, high + 1):
                    block = jnp.where(where == i, src[rows, i * LANES : (i + 1) * LANES], block)
                taken = jnp.take_along_axis(block, slots, axis=1, mode="promise_in_bounds")
                dst[t // X_TILES, rows, lanes] = jnp.where(live, taken, 0.0)

    def remote(src, dst, send, recv, peer):
        return pltpu.make_async_remote_copy(
            src_ref=src, dst_ref=dst, send_sem=send, recv_sem=recv, device_id=peer, device_id_type=MESH
        )

    halos = [
        remote(to_left, from_right, halo_s.at[0], halo_r.at[0], {"tm": left}),
        remote(to_right, from_left, halo_s.at[1], halo_r.at[1], {"tm": right}),
        remote(edge, edge_in, halo_s.at[2], halo_r.at[2], {"tm": right}),
    ]

    def lanes_of(xp):
        return pl.ds(pl.multiple_of(xp * WIDE, LANES), WIDE)

    def x_send(k, p):
        xp, peer = x_peer(k)
        src = xs[p].at[xp] if p else u0.at[:, lanes_of(xp)]
        dst = xr[p].at[mx] if p else w0.at[:, lanes_of(mx)]
        return remote(src, dst, x_s.at[p, xp], x_r.at[p, mx], peer)

    def x_arrival(k, p):
        xp, peer = x_peer(k)
        src = xs[p].at[xp] if p else u0.at[:, lanes_of(xp)]
        dst = xr[p].at[xp] if p else w0.at[:, lanes_of(xp)]
        return remote(src, dst, x_s.at[p, xp], x_r.at[p, xp], peer)

    def z_send(k, p):
        z, peer = z_peer(k)
        return remote(zs[p].at[z], zr[p].at[mz], z_s.at[p, z], z_r.at[p, mz], peer)

    def z_arrival(k, p):
        z, peer = z_peer(k)
        return remote(zs[p].at[z], zr[p].at[z], z_s.at[p, z], z_r.at[p, z], peer)

    def x_out(p):
        for k in X_ORDER:
            x_send(k, p).start()
        if p:
            xr[p][mx] = xs[p][mx]
        else:
            w0[:, lanes_of(mx)] = u0[:, lanes_of(mx)]

    def x_in(p):
        for k in X_ORDER:
            x_arrival(k, p).wait_recv()

    def z_out(p, order):
        for k in order:
            z_send(k, p).start()

    def z_in(p):
        for k in FAR_FIRST:
            z_arrival(k, p).wait_recv()

    def piece(src, xp, strip, z, lane_to):
        rows = slice(8 * strip, 8 * strip + 8)
        begin = z * CAP
        t = begin // LANES
        block = src[xp, rows, t * LANES : (t + 1) * LANES]
        if begin + CAP > (t + 1) * LANES:
            after = src[xp, rows, (t + 1) * LANES : (t + 2) * LANES]
            block = jnp.where(lane >= begin - t * LANES, block, after)
        turn = (lane_to - begin) % LANES
        return pltpu.roll(block, turn, 1) if turn else block

    def joined(src, strip, z):
        out = piece(src, 0, strip, z, 0)
        for xp in range(1, NX):
            out = jnp.where(lane >= xp * CAP, piece(src, xp, strip, z, xp * CAP), out)
        return out

    pl.semaphore_wait(barrier, len(peers))
    halos[0].start()
    halos[1].start()
    for k in NEAR:
        pl.semaphore_signal(far_sem.at[(NZ - k) % NZ], inc=1, device_id=z_peer(k)[1], device_id_type=MESH)

    pack(0)
    for z in range(NZ):
        for i in range(2):
            last = jnp.where(row < 2, piece(xs0, i, 2, z, SPAN), piece(xs0, i + 2, 2, z, SPAN))
            zs0[z, 8 * i : 8 * i + 8, :] = jnp.where(spare, last, joined(xs0, i, z))
    z_out(0, NEAR)
    zr0[mz] = zs0[mz]

    halos[0].wait_recv()
    halos[1].wait_recv()

    for c in range(ROWS // CHUNK):
        lanes = slice(c * CHUNK, (c + 1) * CHUNK)
        x0, d1, e2, e4 = (pair(to_left, i, lanes) for i in range(4))
        d5, x6, x7 = (pair(to_right, i, lanes) for i in range(1, 4))
        x8, d9, e10, e12 = (pair(from_right, i, lanes) for i in range(4))
        em4, dm3, xm2, xm1 = (pair(from_left, i, lanes) for i in range(4))
        dm1 = detail_of(xm2, xm1, x0, 1.0)
        e0 = updated(x0, chosen(first, d1, dm1), d1)
        d7 = detail_of(x6, x7, x8, 1.0, final)
        e6 = updated(x6, d5, d7)
        e8 = updated(x8, d7, d9)
        em2 = updated(xm2, dm3, dm1)
        dm2 = detail_of(em4, em2, e0, 2.0)
        d2 = detail_of(e0, e2, e4, 2.0)
        d6 = detail_of(e4, e6, e8, 2.0, final)
        d10 = detail_of(e8, e10, e12, 2.0)
        f0 = updated(e0, chosen(first, d2, dm2), d2)
        f4 = updated(e4, d2, d6)
        f8 = updated(e8, d6, d10)
        d4 = detail_of(f0, f4, f8, 4.0, final)
        for i, v in enumerate((d2, d7, d6, d4)):
            put(s1, i, lanes, v)
        put(s2, 0, lanes, f0)
        put(edge, 0, lanes, d4)

    halos[2].start()
    pack(1)
    x_out(1)

    for k in FAR:
        if k <= NZ // 2:
            pl.semaphore_wait(far_sem.at[k - REACH], 1)
        if k >= NZ // 2:
            pl.semaphore_wait(far_sem.at[k + REACH], 1)
        z_send(k, 0).start()

    halos[2].wait_recv()
    d4 = edge[...]
    before = jnp.where(first, d4, edge_in[...])
    s2[0:6, :] = s2[0:6, :] + 0.25 * (before + d4)
    pack(2)
    x_out(2)

    x_in(1)
    for z in range(NZ):
        last = joined(xr1, 2, z)
        for i in range(2):
            zs1[z, 8 * i : 8 * i + 8, :] = jnp.where(spare, pltpu.roll(last, SPAN - 32 * i, 1), joined(xr1, i, z))
        zs2[z] = pltpu.roll(last, SPAN - 64, 1)
    z_out(1, FAR_FIRST)
    zr1[mz] = zs1[mz]

    x_in(2)
    for z in range(NZ):
        zs2[z] = jnp.where(spare, zs2[z], joined(xr2, 0, z))
    z_out(2, FAR_FIRST)
    zr2[mz] = zs2[mz]

    def unpack(u, strip, part):
        rows = slice(8 * strip, 8 * strip + 8)
        for xp in range(NX):
            tiles = [None] * X_TILES
            for z in range(NZ):
                block, begin = part(z, xp)
                turn = (z * CAP - begin) % LANES
                turned = pltpu.roll(block, turn, 1) if turn else block
                for t in range(X_TILES):
                    low, high = z * CAP - t * LANES, (z + 1) * CAP - t * LANES
                    if high > 0 and low < LANES:
                        old = tiles[t]
                        tiles[t] = turned if old is None else jnp.where(lane >= low, turned, old)
            for t in range(X_TILES):
                at = (xp * X_TILES + t) * LANES
                u[rows, at : at + LANES] = tiles[t]

    z_in(0)
    for strip in range(2):
        unpack(u0, strip, lambda z, xp: (zr0[z, 8 * strip : 8 * strip + 8, :], xp * CAP))
    unpack(u0, 2, lambda z, xp: (zr0[z, 8 * (xp % 2) : 8 * (xp % 2) + 8, :], SPAN))
    half = NX * WIDE // 2
    u0[16:18, half:] = u0[18:20, half:]
    x_out(0)

    z_in(1)
    for strip in range(2):
        unpack(u1, strip, lambda z, xp: (zr1[z, 8 * strip : 8 * strip + 8, :], xp * CAP))
    coef[2] = u1[0:6, :]
    coef[7] = u1[6:12, :]
    coef[6, 0:4] = u1[12:16, :]
    for z in range(NZ):
        low = pltpu.roll(zr1[z, 0:8, :], 32, 1)
        tail[z] = jnp.where(lane < 32, low, pltpu.roll(zr1[z, 8:16, :], 64, 1))

    z_in(2)
    unpack(u1, 3, lambda z, xp: (zr2[z], xp * CAP))
    coef[0] = u1[24:30, :]
    x_in(0)
    coef[1] = w0[0:6, :]
    coef[3] = w0[6:12, :]
    coef[5] = w0[12:18, :]
    for t in range(SLOT_TILES):
        oid[t : t + 1, :] = u1[30:31, t * LANES : (t + 1) * LANES].astype(jnp.int32) - 1
    for z in range(NZ):
        tail[z] = jnp.where(lane < 64, tail[z], pltpu.roll(zr2[z], 96, 1))
    unpack(u1, 2, lambda z, xp: (tail[z], xp * CAP))
    coef[6, 4:6] = u1[16:18, :]
    coef[4] = u1[18:24, :]

    for halo in halos:
        halo.wait_send()
    for p in range(3):
        for k in X_ORDER:
            x_send(k, p).wait_send()
        for k in FAR_FIRST:
            z_send(k, p).wait_send()


def per_device(trajectory, counts, particle_ids):
    f32, i32 = jnp.float32, jnp.int32
    vmem = lambda *shape: pltpu.VMEM(shape, f32)
    dma = pltpu.SemaphoreType.DMA
    slots = NX * WIDE
    coefficients, owned = pl.pallas_call(
        kernel,
        out_shape=(pltpu.VMEM((8, 6, slots), f32), pltpu.VMEM((SLOT_TILES, LANES), i32)),
        in_specs=[pl.BlockSpec(memory_space=pltpu.HBM)] * 3,
        out_specs=(pl.BlockSpec(memory_space=pltpu.VMEM), pl.BlockSpec(memory_space=pltpu.VMEM)),
        scratch_shapes=[
            pltpu.SMEM((1, NX * NZ), i32), pltpu.VMEM((1, ROWS), i32), vmem(6, 8, ROWS),
            *[vmem(rows, ROWS) for rows, _ in PHASES],
            vmem(24, ROWS), vmem(24, ROWS), vmem(24, ROWS), vmem(24, ROWS),
            vmem(6, ROWS), vmem(6, ROWS),
            pltpu.VMEM((SLOT_TILES, 8, LANES), i32), pltpu.VMEM((SLOT_TILES, 8, LANES), i32),
            pltpu.SMEM((NX * NZ,), i32),
            *[vmem(NX, rows, WIDE) for rows, _ in PHASES],
            *[vmem(NX, rows, WIDE) for rows, _ in PHASES],
            *[vmem(NZ, 8 * tiles, LANES) for _, tiles in PHASES],
            *[vmem(NZ, 8 * tiles, LANES) for _, tiles in PHASES],
            vmem(NZ, 8, LANES), vmem(24, slots), vmem(32, slots), vmem(24, slots),
            dma((3,)), pltpu.SemaphoreType.REGULAR((NZ,)), dma((3,)), dma((3,)),
            dma((3, NZ)), dma((3, NZ)), dma((3, NX)), dma((3, NX)),
        ],
        compiler_params=pltpu.CompilerParams(
            collective_id=0, has_side_effects=True, vmem_limit_bytes=60 * 2**20
        ),
        name="regroup_and_lift",
    )(counts, particle_ids.reshape(1, ROWS), trajectory.transpose(1, 0, 2))
    return coefficients, owned.reshape(slots)


def solution(mesh):
    return jax.shard_map(
        per_device,
        mesh=mesh,
        in_specs=(P("tm", None, "space"), P("space", None), P("space")),
        out_specs=(P("tm", None, "space"), P("space")),
        check_vma=False,
    )
```

time: 42 us -> 38.1 us (0.907)
  the two profiles are of different devices: /device:TPU:16 before, /device:TPU:32 now
where the time goes in v2:
time: 38.1 us; the launch traced here: 37.9 us
  Pallas kernels  35.8 us (94%)
  local copies, waits for them, and re-layouts  1.49 us (4%)
  between operations  0.64 us (2%)
    pallas_call x1, Pallas kernels, per_device(): pl.pallas_call(kernel, out_shape=(pltpu.VMEM((8, 6, slots), f32), pltpu.V...  35.8 us
    unnamed x2, local copies, waits for them, and re-layouts  1.49 us

profile of v2, /device:TPU:32, one launch (start us, length us, event | category | flops | bytes accessed | tf_op | source)
XLA Modules:
  0.0 37.9 jit_solution(12535336747217786750)
XLA Ops:
  0.6 35.8 %regroup_and_lift.1 = (f32[8,6,1536]{2,1,0:T(8,128)S(1)}, s32[12,128]{1,0:T(8,128)S(1)}) custom-call(s32[1,64]{1,0:T(1,128)} %counts_hbm.1, s32[1,1024]{1,0:T(1,128)} %bitcast.5, f32[6,8,1024]{2,1,0:T(8,128)} %bitcast.4), custom_call_target="tpu_custom_call" | custom-call | tf_op jit(solution)/shard_map/regroup_and_lift/pallas_call | solution.py:373
  36.4 0.9 %copy.5 = f32[8,6,1536]{2,0,1:T(8,128)} copy(f32[8,6,1536]{2,1,0:T(8,128)S(1)} %get-tuple-element.6) | data formatting | bytes 589824
  37.3 0.6 %copy.7 = s32[1536]{0:T(1024)} copy(s32[1536]{0:T(1024)S(1)} %bitcast.3) | data formatting | bytes 12288

commit v3 on v2

--- a/solution.py
+++ b/solution.py
@@ -24,7 +24,8 @@
 FAR = (5, 11, 6, 10, 7, 9, 8)
 FAR_FIRST = (8, 7, 9, 6, 10, 5, 11) + NEAR
 SPAN = NX * CAP
-PHASES = ((24, 2), (24, 2), (8, 1))
+PHASES = ((24, 2), (16, 1), (16, 1), (16, 1))
+Z_FIRST = (0, 1)
 
 
 def wrapped(delta):
@@ -52,17 +53,15 @@
 
 def kernel(
     counts_hbm, ids_hbm, traj, coef, oid,
-    counts, ids, x, s0, s1, s2, to_left, to_right, from_right, from_left, edge, edge_in,
-    index, place, offs, xs0, xs1, xs2, xr0, xr1, xr2, zs0, zs1, zs2, zr0, zr1, zr2, tail, u0, u1, w0,
-    load_sem, far_sem, halo_s, halo_r, z_s, z_r, x_s, x_r,
+    counts, ids, x, to_left, to_right, from_right, from_left, edge, edge_in, even, index, place, offs, *refs
 ):
+    rows_of, xs, xr, zs, zr, u, w = (refs[4 * i : 4 * i + 4] for i in range(7))
+    load_sem, far_sem, halo_s, halo_r, z_s, z_r, x_s, x_r = refs[28:]
     me = lax.axis_index("space")
     mx, mz = me // NZ, me % NZ
     mt = lax.axis_index("tm")
     first, final = mt == 0, mt == NT - 1
     left, right = (mt + NT - 1) % NT, (mt + 1) % NT
-    rows_of, xs, xr = (s0, s1, s2), (xs0, xs1, xs2), (xr0, xr1, xr2)
-    zs, zr = (zs0, zs1, zs2), (zr0, zr1, zr2)
 
     def z_peer(k):
         z = (mz + k) % NZ
@@ -135,11 +134,21 @@
         for i, v in enumerate((e4, d5, p[6], p[7])):
             put(to_right, i, lanes, v)
         for i, v in enumerate((d1, d3, d5)):
-            put(s0, i, lanes, v)
-        s0[18:20, lanes] = d5[1][1:3]
-        s0[20:24, lanes] = jnp.zeros((4, CHUNK), jnp.float32)
-        s2[6:7, lanes] = (ids[0:1, lanes] + 1).astype(jnp.float32)
-        s2[7:8, lanes] = jnp.zeros((1, CHUNK), jnp.float32)
+            put(rows_of[0], i, lanes, v)
+        tag = (ids[0:1, lanes] + 1).astype(jnp.float32)
+        rows_of[0][18:19, lanes] = tag
+        rows_of[0][20:22, lanes] = d5[1][1:3]
+        rows_of[0][22:23, lanes] = tag
+
+    def spread(r, lanes, value):
+        n = value.shape[0]
+        i = 0
+        while i < n:
+            dst, at = rows_of[1 + (r + i) // 10], (r + i) % 10
+            m = min(n - i, (8 if at < 8 else 10) - at)
+            for again in range(1 if at < 8 else NX):
+                dst[at + 2 * again : at + 2 * again + m, lanes] = value[i : i + m]
+            i += m
 
     def pack(phase):
         src, dst = rows_of[phase], xs[phase]
@@ -174,16 +183,19 @@
     def lanes_of(xp):
         return pl.ds(pl.multiple_of(xp * WIDE, LANES), WIDE)
 
+    def x_refs(p, there, here):
+        if p in Z_FIRST:
+            return u[p].at[:, lanes_of(there)], w[p].at[:, lanes_of(here)]
+        return xs[p].at[there], xr[p].at[here]
+
     def x_send(k, p):
         xp, peer = x_peer(k)
-        src = xs[p].at[xp] if p else u0.at[:, lanes_of(xp)]
-        dst = xr[p].at[mx] if p else w0.at[:, lanes_of(mx)]
+        src, dst = x_refs(p, xp, mx)
         return remote(src, dst, x_s.at[p, xp], x_r.at[p, mx], peer)
 
     def x_arrival(k, p):
         xp, peer = x_peer(k)
-        src = xs[p].at[xp] if p else u0.at[:, lanes_of(xp)]
-        dst = xr[p].at[xp] if p else w0.at[:, lanes_of(xp)]
+        src, dst = x_refs(p, xp, xp)
         return remote(src, dst, x_s.at[p, xp], x_r.at[p, xp], peer)
 
     def z_send(k, p):
@@ -197,10 +209,10 @@
     def x_out(p):
         for k in X_ORDER:
             x_send(k, p).start()
-        if p:
+        if p in Z_FIRST:
+            w[p][:, lanes_of(mx)] = u[p][:, lanes_of(mx)]
+        else:
             xr[p][mx] = xs[p][mx]
-        else:
-            w0[:, lanes_of(mx)] = u0[:, lanes_of(mx)]
 
     def x_in(p):
         for k in X_ORDER:
@@ -208,27 +220,36 @@
 
     def z_out(p, order):
         for k in order:
+            if p == 0 and k in FAR:
+                if k <= NZ // 2:
+                    pl.semaphore_wait(far_sem.at[k - REACH], 1)
+                if k >= NZ // 2:
+                    pl.semaphore_wait(far_sem.at[k + REACH], 1)
             z_send(k, p).start()
 
     def z_in(p):
         for k in FAR_FIRST:
             z_arrival(k, p).wait_recv()
 
-    def piece(src, xp, strip, z, lane_to):
+    def blocks_of(src, strip):
         rows = slice(8 * strip, 8 * strip + 8)
+        return [
+            [src[xp, rows, t * LANES : (t + 1) * LANES] for t in range(X_TILES)] for xp in range(NX)
+        ]
+
+    def piece(blocks, xp, z, lane_to):
         begin = z * CAP
         t = begin // LANES
-        block = src[xp, rows, t * LANES : (t + 1) * LANES]
+        block = blocks[xp][t]
         if begin + CAP > (t + 1) * LANES:
-            after = src[xp, rows, (t + 1) * LANES : (t + 2) * LANES]
-            block = jnp.where(lane >= begin - t * LANES, block, after)
+            block = jnp.where(lane >= begin - t * LANES, block, blocks[xp][t + 1])
         turn = (lane_to - begin) % LANES
         return pltpu.roll(block, turn, 1) if turn else block
 
-    def joined(src, strip, z):
-        out = piece(src, 0, strip, z, 0)
+    def joined(blocks, z):
+        out = piece(blocks, 0, z, 0)
         for xp in range(1, NX):
-            out = jnp.where(lane >= xp * CAP, piece(src, xp, strip, z, xp * CAP), out)
+            out = jnp.where(lane >= xp * CAP, piece(blocks, xp, z, xp * CAP), out)
         return out
 
     pl.semaphore_wait(barrier, len(peers))
@@ -237,13 +258,25 @@
     for k in NEAR:
         pl.semaphore_signal(far_sem.at[(NZ - k) % NZ], inc=1, device_id=z_peer(k)[1], device_id_type=MESH)
 
+    def join(p, src):
+        tiles = PHASES[p][1]
+        per = NX // tiles
+        last = blocks_of(src, tiles)
+        for i in range(tiles):
+            blocks = blocks_of(src, i)
+            for z in range(NZ):
+                more = piece(last, i, z, SPAN)
+                for j in range(1, per):
+                    more = jnp.where(row < 8 // per * j, more, piece(last, i + tiles * j, z, SPAN))
+                zs[p][z, 8 * i : 8 * i + 8, :] = jnp.where(spare, more, joined(blocks, z))
+
+    def own_z(p):
+        zr[p][mz] = zs[p][mz]
+
     pack(0)
-    for z in range(NZ):
-        for i in range(2):
-            last = jnp.where(row < 2, piece(xs0, i, 2, z, SPAN), piece(xs0, i + 2, 2, z, SPAN))
-            zs0[z, 8 * i : 8 * i + 8, :] = jnp.where(spare, last, joined(xs0, i, z))
+    join(0, xs[0])
     z_out(0, NEAR)
-    zr0[mz] = zs0[mz]
+    z_out(0, FAR[:4])
 
     halos[0].wait_recv()
     halos[1].wait_recv()
@@ -268,50 +301,43 @@
         f4 = updated(e4, d2, d6)
         f8 = updated(e8, d6, d10)
         d4 = detail_of(f0, f4, f8, 4.0, final)
-        for i, v in enumerate((d2, d7, d6, d4)):
-            put(s1, i, lanes, v)
-        put(s2, 0, lanes, f0)
+        for i, v in enumerate((d7, d6, d2, d4)):
+            spread(6 * i, lanes, v[0])
+            spread(6 * i + 3, lanes, v[1])
+        put(even, 0, lanes, f0)
         put(edge, 0, lanes, d4)
 
     halos[2].start()
+    pack(2)
+    x_out(2)
+    z_out(0, FAR[4:])
     pack(1)
-    x_out(1)
-
-    for k in FAR:
-        if k <= NZ // 2:
-            pl.semaphore_wait(far_sem.at[k - REACH], 1)
-        if k >= NZ // 2:
-            pl.semaphore_wait(far_sem.at[k + REACH], 1)
-        z_send(k, 0).start()
+    join(1, xs[1])
+    z_out(1, FAR_FIRST)
+    own_z(0)
+    own_z(1)
 
     halos[2].wait_recv()
     d4 = edge[...]
     before = jnp.where(first, d4, edge_in[...])
-    s2[0:6, :] = s2[0:6, :] + 0.25 * (before + d4)
-    pack(2)
-    x_out(2)
-
-    x_in(1)
-    for z in range(NZ):
-        last = joined(xr1, 2, z)
-        for i in range(2):
-            zs1[z, 8 * i : 8 * i + 8, :] = jnp.where(spare, pltpu.roll(last, SPAN - 32 * i, 1), joined(xr1, i, z))
-        zs2[z] = pltpu.roll(last, SPAN - 64, 1)
-    z_out(1, FAR_FIRST)
-    zr1[mz] = zs1[mz]
+    spread(24, slice(None), even[...] + 0.25 * (before + d4))
+    pack(3)
+    x_out(3)
 
     x_in(2)
-    for z in range(NZ):
-        zs2[z] = jnp.where(spare, zs2[z], joined(xr2, 0, z))
+    join(2, xr[2])
     z_out(2, FAR_FIRST)
-    zr2[mz] = zs2[mz]
-
-    def unpack(u, strip, part):
-        rows = slice(8 * strip, 8 * strip + 8)
+    own_z(2)
+    x_in(3)
+    join(3, xr[3])
+    z_out(3, FAR_FIRST)
+    own_z(3)
+
+    def unpack(dst, at, n, part):
         for xp in range(NX):
             tiles = [None] * X_TILES
             for z in range(NZ):
-                block, begin = part(z, xp)
+                block, begin, skip = part(z, xp)
                 turn = (z * CAP - begin) % LANES
                 turned = pltpu.roll(block, turn, 1) if turn else block
                 for t in range(X_TILES):
@@ -320,45 +346,51 @@
                         old = tiles[t]
                         tiles[t] = turned if old is None else jnp.where(lane >= low, turned, old)
             for t in range(X_TILES):
-                at = (xp * X_TILES + t) * LANES
-                u[rows, at : at + LANES] = tiles[t]
+                lanes = slice((xp * X_TILES + t) * LANES, (xp * X_TILES + t + 1) * LANES)
+                dst[at : at + n, lanes] = tiles[t][skip : skip + n]
+
+    def unjoin(p, few):
+        tiles = PHASES[p][1]
+        per = NX // tiles
+        for i in range(tiles):
+            unpack(u[p], 8 * i, 8, lambda z, xp: (zr[p][z, 8 * i : 8 * i + 8, :], xp * CAP, 0))
+
+        def rest(z, xp):
+            i = xp % tiles
+            return zr[p][z, 8 * i : 8 * i + 8, :], SPAN, 8 // per * (xp // tiles)
+
+        unpack(u[p], 8 * tiles, few, rest)
 
     z_in(0)
-    for strip in range(2):
-        unpack(u0, strip, lambda z, xp: (zr0[z, 8 * strip : 8 * strip + 8, :], xp * CAP))
-    unpack(u0, 2, lambda z, xp: (zr0[z, 8 * (xp % 2) : 8 * (xp % 2) + 8, :], SPAN))
-    half = NX * WIDE // 2
-    u0[16:18, half:] = u0[18:20, half:]
+    unjoin(0, 3)
     x_out(0)
-
     z_in(1)
-    for strip in range(2):
-        unpack(u1, strip, lambda z, xp: (zr1[z, 8 * strip : 8 * strip + 8, :], xp * CAP))
-    coef[2] = u1[0:6, :]
-    coef[7] = u1[6:12, :]
-    coef[6, 0:4] = u1[12:16, :]
-    for z in range(NZ):
-        low = pltpu.roll(zr1[z, 0:8, :], 32, 1)
-        tail[z] = jnp.where(lane < 32, low, pltpu.roll(zr1[z, 8:16, :], 64, 1))
+    unjoin(1, 2)
+    x_out(1)
 
     z_in(2)
-    unpack(u1, 3, lambda z, xp: (zr2[z], xp * CAP))
-    coef[0] = u1[24:30, :]
+    unjoin(2, 2)
+    coef[6, 4:6] = u[2][0:2, :]
+    coef[2] = u[2][2:8, :]
+    coef[4, 0:2] = u[2][8:10, :]
     x_in(0)
-    coef[1] = w0[0:6, :]
-    coef[3] = w0[6:12, :]
-    coef[5] = w0[12:18, :]
+    coef[1] = w[0][0:6, :]
+    coef[3] = w[0][6:12, :]
+    coef[5] = w[0][12:18, :]
     for t in range(SLOT_TILES):
-        oid[t : t + 1, :] = u1[30:31, t * LANES : (t + 1) * LANES].astype(jnp.int32) - 1
-    for z in range(NZ):
-        tail[z] = jnp.where(lane < 64, tail[z], pltpu.roll(zr2[z], 96, 1))
-    unpack(u1, 2, lambda z, xp: (tail[z], xp * CAP))
-    coef[6, 4:6] = u1[16:18, :]
-    coef[4] = u1[18:24, :]
+        oid[t : t + 1, :] = w[0][18:19, t * LANES : (t + 1) * LANES].astype(jnp.int32) - 1
+    x_in(1)
+    coef[7] = w[1][0:6, :]
+    coef[6, 0:4] = w[1][6:10, :]
+
+    z_in(3)
+    unjoin(3, 2)
+    coef[4, 2:6] = u[3][0:4, :]
+    coef[0] = u[3][4:10, :]
 
     for halo in halos:
         halo.wait_send()
-    for p in range(3):
+    for p in range(len(PHASES)):
         for k in X_ORDER:
             x_send(k, p).wait_send()
         for k in FAR_FIRST:
@@ -377,18 +409,19 @@
         out_specs=(pl.BlockSpec(memory_space=pltpu.VMEM), pl.BlockSpec(memory_space=pltpu.VMEM)),
         scratch_shapes=[
             pltpu.SMEM((1, NX * NZ), i32), pltpu.VMEM((1, ROWS), i32), vmem(6, 8, ROWS),
-            *[vmem(rows, ROWS) for rows, _ in PHASES],
             vmem(24, ROWS), vmem(24, ROWS), vmem(24, ROWS), vmem(24, ROWS),
-            vmem(6, ROWS), vmem(6, ROWS),
+            vmem(6, ROWS), vmem(6, ROWS), vmem(6, ROWS),
             pltpu.VMEM((SLOT_TILES, 8, LANES), i32), pltpu.VMEM((SLOT_TILES, 8, LANES), i32),
             pltpu.SMEM((NX * NZ,), i32),
+            *[vmem(rows, ROWS) for rows, _ in PHASES],
             *[vmem(NX, rows, WIDE) for rows, _ in PHASES],
             *[vmem(NX, rows, WIDE) for rows, _ in PHASES],
             *[vmem(NZ, 8 * tiles, LANES) for _, tiles in PHASES],
             *[vmem(NZ, 8 * tiles, LANES) for _, tiles in PHASES],
-            vmem(NZ, 8, LANES), vmem(24, slots), vmem(32, slots), vmem(24, slots),
+            *[vmem(rows, slots) for rows, _ in PHASES],
+            *[vmem(rows, slots) for rows, _ in PHASES],
             dma((3,)), pltpu.SemaphoreType.REGULAR((NZ,)), dma((3,)), dma((3,)),
-            dma((3, NZ)), dma((3, NZ)), dma((3, NX)), dma((3, NX)),
+            dma((4, NZ)), dma((4, NZ)), dma((4, NX)), dma((4, NX)),
         ],
         compiler_params=pltpu.CompilerParams(
             collective_id=0, has_side_effects=True, vmem_limit_bytes=60 * 2**20

time: 38.1 us -> 35.5 us (0.932)
  the two profiles are of different devices: /device:TPU:32 before, /device:TPU:2 now
where the time goes in v3:
time: 35.5 us; the launch traced here: 35.3 us
  Pallas kernels  33.1 us (93%)
  local copies, waits for them, and re-layouts  1.49 us (4%)
  between operations  0.64 us (2%)
    pallas_call x1, Pallas kernels, per_device(): pl.pallas_call(kernel, out_shape=(pltpu.VMEM((8, 6, slots), f32), pltpu.V...  33.1 us
    unnamed x2, local copies, waits for them, and re-layouts  1.49 us

profile of v3, /device:TPU:2, one launch (start us, length us, event | category | flops | bytes accessed | tf_op | source)
XLA Modules:
  0.0 35.3 jit_solution(815575951028479030)
XLA Ops:
  0.6 33.1 %regroup_and_lift.1 = (f32[8,6,1536]{2,1,0:T(8,128)S(1)}, s32[12,128]{1,0:T(8,128)S(1)}) custom-call(s32[1,64]{1,0:T(1,128)} %counts_hbm.1, s32[1,1024]{1,0:T(1,128)} %bitcast.5, f32[6,8,1024]{2,1,0:T(8,128)} %bitcast.4), custom_call_target="tpu_custom_call" | custom-call | tf_op jit(solution)/shard_map/regroup_and_lift/pallas_call | solution.py:405
  33.8 0.9 %copy.5 = f32[8,6,1536]{2,0,1:T(8,128)} copy(f32[8,6,1536]{2,1,0:T(8,128)S(1)} %get-tuple-element.6) | data formatting | bytes 589824
  34.7 0.6 %copy.7 = s32[1536]{0:T(1024)} copy(s32[1536]{0:T(1024)S(1)} %bitcast.3) | data formatting | bytes 12288

commit v4 on v3

--- a/solution.py
+++ b/solution.py
@@ -227,6 +227,11 @@
                     pl.semaphore_wait(far_sem.at[k + REACH], 1)
             z_send(k, p).start()
 
+    def z_part(p, low, high, order=FAR_FIRST):
+        for k in order:
+            z = (mz + k) % NZ
+            pl.when((z >= low) & (z < high))(lambda k=k: z_send(k, p).start())
+
     def z_in(p):
         for k in FAR_FIRST:
             z_arrival(k, p).wait_recv()
@@ -253,10 +258,11 @@
         return out
 
     pl.semaphore_wait(barrier, len(peers))
+    for k in NEAR:
+        pl.semaphore_signal(far_sem.at[(NZ - k) % NZ], inc=1, device_id=z_peer(k)[1], device_id_type=MESH)
+
     halos[0].start()
     halos[1].start()
-    for k in NEAR:
-        pl.semaphore_signal(far_sem.at[(NZ - k) % NZ], inc=1, device_id=z_peer(k)[1], device_id_type=MESH)
 
     def join(p, src):
         tiles = PHASES[p][1]
@@ -276,7 +282,7 @@
     pack(0)
     join(0, xs[0])
     z_out(0, NEAR)
-    z_out(0, FAR[:4])
+    z_out(0, FAR[:6])
 
     halos[0].wait_recv()
     halos[1].wait_recv()
@@ -310,10 +316,11 @@
     halos[2].start()
     pack(2)
     x_out(2)
-    z_out(0, FAR[4:])
+    z_out(0, FAR[6:])
     pack(1)
     join(1, xs[1])
-    z_out(1, FAR_FIRST)
+    z_part(1, 0, 4)
+    z_part(1, 4, 16)
     own_z(0)
     own_z(1)
 
@@ -326,11 +333,16 @@
 
     x_in(2)
     join(2, xr[2])
-    z_out(2, FAR_FIRST)
+    z_part(2, 0, 4)
     own_z(2)
     x_in(3)
     join(3, xr[3])
-    z_out(3, FAR_FIRST)
+    z_part(3, 0, 2)
+    z_part(3, 2, 4)
+    z_part(2, 4, 16, FAR_FIRST[:7])
+    z_part(3, 4, 16, FAR_FIRST[:7])
+    z_part(2, 4, 16, NEAR)
+    z_part(3, 4, 16, NEAR)
     own_z(3)
 
     def unpack(dst, at, n, part):
@@ -370,23 +382,23 @@
 
     z_in(2)
     unjoin(2, 2)
-    coef[6, 4:6] = u[2][0:2, :]
-    coef[2] = u[2][2:8, :]
-    coef[4, 0:2] = u[2][8:10, :]
+    coef[4:6, 6, :] = u[2][0:2, :]
+    coef[0:6, 2, :] = u[2][2:8, :]
+    coef[0:2, 4, :] = u[2][8:10, :]
     x_in(0)
-    coef[1] = w[0][0:6, :]
-    coef[3] = w[0][6:12, :]
-    coef[5] = w[0][12:18, :]
+    coef[0:6, 1, :] = w[0][0:6, :]
+    coef[0:6, 3, :] = w[0][6:12, :]
+    coef[0:6, 5, :] = w[0][12:18, :]
     for t in range(SLOT_TILES):
         oid[t : t + 1, :] = w[0][18:19, t * LANES : (t + 1) * LANES].astype(jnp.int32) - 1
     x_in(1)
-    coef[7] = w[1][0:6, :]
-    coef[6, 0:4] = w[1][6:10, :]
+    coef[0:6, 7, :] = w[1][0:6, :]
+    coef[0:4, 6, :] = w[1][6:10, :]
 
     z_in(3)
     unjoin(3, 2)
-    coef[4, 2:6] = u[3][0:4, :]
-    coef[0] = u[3][4:10, :]
+    coef[2:6, 4, :] = u[3][0:4, :]
+    coef[0:6, 0, :] = u[3][4:10, :]
 
     for halo in halos:
         halo.wait_send()
@@ -404,7 +416,7 @@
     slots = NX * WIDE
     coefficients, owned = pl.pallas_call(
         kernel,
-        out_shape=(pltpu.VMEM((8, 6, slots), f32), pltpu.VMEM((SLOT_TILES, LANES), i32)),
+        out_shape=(pltpu.VMEM((6, 8, slots), f32), pltpu.VMEM((SLOT_TILES, LANES), i32)),
         in_specs=[pl.BlockSpec(memory_space=pltpu.HBM)] * 3,
         out_specs=(pl.BlockSpec(memory_space=pltpu.VMEM), pl.BlockSpec(memory_space=pltpu.VMEM)),
         scratch_shapes=[
@@ -428,7 +440,7 @@
         ),
         name="regroup_and_lift",
     )(counts, particle_ids.reshape(1, ROWS), trajectory.transpose(1, 0, 2))
-    return coefficients, owned.reshape(slots)
+    return coefficients.transpose(1, 0, 2), owned.reshape(slots)
 
 
 def solution(mesh):

time: 35.5 us -> 34.5 us (0.972)
  Pallas kernels: 33.1 us -> 32.4 us
    pallas_call x1, Pallas kernels: 33.1 us -> 32.4 us  [per_device(): pl.pallas_call(kernel, out_shape=(pltpu.VMEM((6, 8, slots), f32), pltpu.V...]
where the time goes in v4:
time: 34.5 us; the launch traced here: 34.4 us
  Pallas kernels  32.4 us (94%)
  local copies, waits for them, and re-layouts  1.32 us (4%)
  between operations  0.64 us (2%)
    pallas_call x1, Pallas kernels, per_device(): pl.pallas_call(kernel, out_shape=(pltpu.VMEM((6, 8, slots), f32), pltpu.V...  32.4 us
    unnamed x2, local copies, waits for them, and re-layouts  1.32 us

profile of v4, /device:TPU:2, one launch (start us, length us, event | category | flops | bytes accessed | tf_op | source)
XLA Modules:
  0.0 34.4 jit_solution(999790868174006324)
XLA Ops:
  0.6 32.4 %regroup_and_lift.1 = (f32[6,8,1536]{2,1,0:T(8,128)S(1)}, s32[12,128]{1,0:T(8,128)S(1)}) custom-call(s32[1,64]{1,0:T(1,128)} %counts_hbm.1, s32[1,1024]{1,0:T(1,128)} %bitcast.7, f32[6,8,1024]{2,1,0:T(8,128)} %bitcast.6), custom_call_target="tpu_custom_call" | custom-call | tf_op jit(solution)/shard_map/regroup_and_lift/pallas_call | solution.py:417
  33.1 0.7 %copy.7 = f32[8,6,1536]{2,0,1:T(8,128)} copy(f32[8,6,1536]{2,0,1:T(8,128)S(1)} %bitcast.4) | data formatting | bytes 589824
  33.8 0.6 %copy.8 = s32[1536]{0:T(1024)} copy(s32[1536]{0:T(1024)S(1)} %bitcast.5) | data formatting | bytes 12288

commit v5 on v4

--- a/solution.py
+++ b/solution.py
@@ -257,13 +257,6 @@
             out = jnp.where(lane >= xp * CAP, piece(blocks, xp, z, xp * CAP), out)
         return out
 
-    pl.semaphore_wait(barrier, len(peers))
-    for k in NEAR:
-        pl.semaphore_signal(far_sem.at[(NZ - k) % NZ], inc=1, device_id=z_peer(k)[1], device_id_type=MESH)
-
-    halos[0].start()
-    halos[1].start()
-
     def join(p, src):
         tiles = PHASES[p][1]
         per = NX // tiles
@@ -281,6 +274,13 @@
 
     pack(0)
     join(0, xs[0])
+    pl.semaphore_wait(barrier, len(peers))
+    halos[0].start()
+    halos[1].start()
+    for k in NEAR:
+        pl.semaphore_signal(far_sem.at[(NZ - k) % NZ], inc=1, device_id=z_peer(k)[1], device_id_type=MESH)
+
+
     z_out(0, NEAR)
     z_out(0, FAR[:6])
 

time: 34.5 us -> 34.5 us (level)
  no operation moved by 1% of the time
where the time goes in v5:
time: 34.5 us; the launch traced here: 34.4 us
  Pallas kernels  32.4 us (94%)
  local copies, waits for them, and re-layouts  1.32 us (4%)
  between operations  0.64 us (2%)
    pallas_call x1, Pallas kernels, per_device(): pl.pallas_call(kernel, out_shape=(pltpu.VMEM((6, 8, slots), f32), pltpu.V...  32.4 us
    unnamed x2, local copies, waits for them, and re-layouts  1.32 us

profile of v5, /device:TPU:2, one launch (start us, length us, event | category | flops | bytes accessed | tf_op | source)
XLA Modules:
  0.0 34.4 jit_solution(15532555141859380447)
XLA Ops:
  0.6 32.4 %regroup_and_lift.1 = (f32[6,8,1536]{2,1,0:T(8,128)S(1)}, s32[12,128]{1,0:T(8,128)S(1)}) custom-call(s32[1,64]{1,0:T(1,128)} %counts_hbm.1, s32[1,1024]{1,0:T(1,128)} %bitcast.7, f32[6,8,1024]{2,1,0:T(8,128)} %bitcast.6), custom_call_target="tpu_custom_call" | custom-call | tf_op jit(solution)/shard_map/regroup_and_lift/pallas_call | solution.py:417
  33.0 0.7 %copy.7 = f32[8,6,1536]{2,0,1:T(8,128)} copy(f32[8,6,1536]{2,0,1:T(8,128)S(1)} %bitcast.4) | data formatting | bytes 589824
  33.8 0.6 %copy.8 = s32[1536]{0:T(1024)} copy(s32[1536]{0:T(1024)S(1)} %bitcast.5) | data formatting | bytes 12288

commit v6 on v5

--- a/solution.py
+++ b/solution.py
@@ -17,7 +17,7 @@
 SLOT_TILES = NX * NZ * CAP // LANES
 WIDE = NZ * CAP
 X_TILES = WIDE // LANES
-CHUNK = 256
+CHUNK = 128
 X_ORDER = (2, 1, 3)
 REACH = 4
 NEAR = (4, 12, 3, 13, 2, 14, 1, 15)

time: 34.5 us -> 34.5 us (level)
  no operation moved by 1% of the time
where the time goes in v6:
time: 34.5 us; the launch traced here: 34.4 us
  Pallas kernels  32.4 us (94%)
  local copies, waits for them, and re-layouts  1.32 us (4%)
  between operations  0.64 us (2%)
    pallas_call x1, Pallas kernels, per_device(): pl.pallas_call(kernel, out_shape=(pltpu.VMEM((6, 8, slots), f32), pltpu.V...  32.4 us
    unnamed x2, local copies, waits for them, and re-layouts  1.32 us

profile of v6, /device:TPU:2, one launch (start us, length us, event | category | flops | bytes accessed | tf_op | source)
XLA Modules:
  0.0 34.4 jit_solution(12462155930752540263)
XLA Ops:
  0.6 32.4 %regroup_and_lift.1 = (f32[6,8,1536]{2,1,0:T(8,128)S(1)}, s32[12,128]{1,0:T(8,128)S(1)}) custom-call(s32[1,64]{1,0:T(1,128)} %counts_hbm.1, s32[1,1024]{1,0:T(1,128)} %bitcast.7, f32[6,8,1024]{2,1,0:T(8,128)} %bitcast.6), custom_call_target="tpu_custom_call" | custom-call | tf_op jit(solution)/shard_map/regroup_and_lift/pallas_call | solution.py:417
  33.0 0.7 %copy.7 = f32[8,6,1536]{2,0,1:T(8,128)} copy(f32[8,6,1536]{2,0,1:T(8,128)S(1)} %bitcast.4) | data formatting | bytes 589824
  33.8 0.6 %copy.8 = s32[1536]{0:T(1024)} copy(s32[1536]{0:T(1024)S(1)} %bitcast.5) | data formatting | bytes 12288
